TPU v7x, 512 devices: a whole 4x8x8 slice. The times are simulated.
512 devices in a mesh: section: 8 (over z_hi, x), tensor: 64 (over y, z_lo, core).
Axes of the slice: x: 4, y: 8, z: 8 (z_hi: 2, z_lo: 4; z = z_hi * 4 + z_lo), core: 2. Of those that a mesh axis runs over, the one named last changes fastest.
Arguments:
- activations: bfloat16 [8, 1024, 8192], P('section', None, 'tensor'), may hold values from -6 to 6
- conv_weight: bfloat16 [8, 4, 8192], P('section', None, 'tensor'), may hold values from -3 to 3
- step_size: float32 [8, 1024, 128], P('section', None, 'tensor'), may hold values from 0.01 to 0.1
- decay_rate: float32 [8, 128], P('section', 'tensor'), may hold values from 0.005 to 1
- skip_gain: float32 [8, 128], P('section', 'tensor'), may hold values from 0.5 to 1.5
- b_matrix: bfloat16 [8, 4, 256, 2048], P('section', None, 'tensor'), may hold values from -0.375 to 0.375
- c_matrix: bfloat16 [8, 4, 256, 2048], P('section', None, 'tensor'), may hold values from -6 to 6
- top_grad: bfloat16 [4, 256, 8192], P(None, 'tensor'), may hold values from -6 to 6
Outputs:
- stream_grad: bfloat16 [8, 4, 256, 8192], P('section', None, 'tensor')
- conv_grad: float32 [8, 4, 8192], P('section', None, 'tensor')
All inputs are finite; a program needn't handle non-finite values.
Results may differ from a plain program's by a relative error of at most 0.035.
Values may be sent and summed in bfloat16 or wider, within the bound.
A program may use at most 128 MiB of HBM per device.

v0:
```python
import jax
import jax.numpy as jnp
from jax import lax
from jax.sharding import PartitionSpec as P

H = 128
P_SIZE = 64
N = 256
K = 4
BLOCKS = 4
CL = 256


def as_sent(array):
    return jax.tree.map(lambda a: a.astype(jnp.bfloat16) if a.dtype == jnp.float32 else a, array)


def passed_along(array, axis, by):
    devices = lax.axis_size(axis)
    pairs = [(i, i + by) for i in range(devices) if 0 <= i + by < devices]
    return lax.ppermute(array, axis, pairs)


def on_device(
    activations, conv_weight, step_size, decay_rate, skip_gain, b_matrix, c_matrix, top_grad
):
    tensor_size = lax.axis_size("tensor")
    section_count = lax.axis_size("section")
    section_pos = lax.axis_index("section")
    heads_local = H // tensor_size
    width_local = heads_local * P_SIZE
    rows_local = CL // tensor_size
    groups = b_matrix.shape[-1] // N
    length = BLOCKS * CL
    inputs = activations[0].astype(jnp.float32)
    weights = conv_weight[0].astype(jnp.float32)
    padded = jnp.concatenate([jnp.zeros((K - 1, width_local), jnp.float32), inputs], axis=0)
    preact = jnp.zeros((length, width_local), jnp.float32)
    for tap_index in range(K):
        preact = (
            preact + weights[tap_index] * padded[K - 1 - tap_index : K - 1 - tap_index + length]
        )
    logistic = jax.nn.sigmoid(preact)
    slope = logistic * (1.0 + preact * (1.0 - logistic))
    step_rows = step_size[0].reshape(BLOCKS, CL, heads_local)
    decay_all = jnp.cumsum(-step_rows * decay_rate[0][None, None, :], axis=1)
    skip_row = skip_gain[0]

    def widen_groups(values):
        spread = values[0].reshape(BLOCKS, rows_local, groups, N)
        spread = jnp.repeat(spread, tensor_size // groups, axis=2)
        return spread.reshape(BLOCKS, rows_local, tensor_size * N)

    b_heads, c_heads = (
        lax.all_to_all(widen_groups(b_matrix), "tensor", split_axis=2, concat_axis=1, tiled=True),
        lax.all_to_all(widen_groups(c_matrix), "tensor", split_axis=2, concat_axis=1, tiled=True),
    )
    causal = jnp.arange(CL)[:, None] >= jnp.arange(CL)[None, :]

    def block_back(block_at, grad_out, carried, window_rows):
        decay_sum = decay_all[block_at]
        decay_end = decay_sum[-1]
        step_block = step_rows[block_at]
        b_block = b_heads[block_at]
        c_block = c_heads[block_at]
        scores = jnp.einsum("jn,in->ji", c_block, b_block, preferred_element_type=jnp.float32)
        decay_t = decay_sum.T
        decay_gap = decay_t[:, :, None] - decay_t[:, None, :]
        factor = jnp.exp(jnp.where(causal[None], decay_gap, 0.0))
        weight = jnp.where(
            causal[None], factor * scores[None] * step_block.T[:, None, :], 0.0
        ).astype(jnp.bfloat16)
        grad_heads = grad_out.reshape(CL, heads_local, P_SIZE)
        inside = jnp.einsum("hji,jhp->ihp", weight, grad_heads, preferred_element_type=jnp.float32)
        through = jnp.einsum(
            "in,hnp->ihp", b_block, carried.astype(jnp.bfloat16), preferred_element_type=jnp.float32
        )
        factor_in = step_block * jnp.exp(decay_end[None, :] - decay_sum)
        grad_mix = (
            inside
            + factor_in[:, :, None] * through
            + skip_row[None, :, None] * grad_heads.astype(jnp.float32)
        )
        scaled = (jnp.exp(decay_sum)[:, :, None] * c_block.astype(jnp.float32)[:, None, :]).astype(
            jnp.bfloat16
        )
        updated = jnp.exp(decay_end)[:, None, None] * carried + jnp.einsum(
            "ihn,ihp->hnp", scaled, grad_heads, preferred_element_type=jnp.float32
        )
        grad_pre = grad_mix.reshape(CL, width_local) * lax.dynamic_slice_in_dim(
            slope, block_at * CL, CL, 0
        )
        extended = jnp.concatenate([grad_pre, window_rows], axis=0)
        act_window = lax.dynamic_slice_in_dim(padded, block_at * CL, CL + K - 1, 0)
        grad_in = jnp.zeros((CL, width_local), jnp.float32)
        conv_rows = []
        for tap_index in range(K):
            grad_in = grad_in + weights[tap_index] * extended[tap_index : tap_index + CL]
            conv_rows.append(
                jnp.sum(grad_pre * act_window[K - 1 - tap_index : K - 1 - tap_index + CL], axis=0)
            )
        return (grad_in.astype(jnp.bfloat16), updated, grad_pre[: K - 1], jnp.stack(conv_rows))

    zero_state = jnp.zeros((heads_local, N, P_SIZE), jnp.float32)
    zero_rows = jnp.zeros((K - 1, width_local), jnp.float32)
    zero_conv = jnp.zeros((K, width_local), jnp.float32)
    grad_top = lax.all_to_all(top_grad, "tensor", split_axis=2, concat_axis=1, tiled=True)

    def whole_layer(upstream):
        carried = zero_state
        window_rows = zero_rows
        conv_sum = zero_conv
        pieces = [None] * BLOCKS
        for block_at in range(BLOCKS - 1, -1, -1):
            grad_in, carried, window_rows, conv_term = block_back(
                block_at, upstream[block_at], carried, window_rows
            )
            pieces[block_at] = (
                upstream[block_at].astype(jnp.float32) + grad_in.astype(jnp.float32)
            ).astype(jnp.bfloat16)
            conv_sum = conv_sum + conv_term
        return (jnp.stack(pieces), conv_sum)

    def pass_through(upstream):
        return (upstream, zero_conv)

    received = jnp.zeros_like(grad_top)
    stream_heads = jnp.zeros_like(grad_top)
    conv_out = zero_conv
    for turn_no in range(section_count):
        active = section_pos == section_count - 1 - turn_no
        upstream = jnp.where(section_pos == section_count - 1, grad_top, received)
        grad_stream, conv_sum = lax.cond(active, whole_layer, pass_through, upstream)
        stream_heads = jnp.where(active, grad_stream, stream_heads)
        conv_out = jnp.where(active, conv_sum, conv_out)
        if turn_no + 1 < section_count:
            received = passed_along(as_sent(grad_stream), "section", -1).astype(grad_stream.dtype)
    stream_out = lax.all_to_all(
        as_sent(stream_heads), "tensor", split_axis=1, concat_axis=2, tiled=True
    ).astype(stream_heads.dtype)
    return (stream_out[None], conv_out[None])


def solution(mesh):
    return jax.shard_map(
        on_device,
        mesh=mesh,
        in_specs=(
            P("section", None, "tensor"),
            P("section", None, "tensor"),
            P("section", None, "tensor"),
            P("section", "tensor"),
            P("section", "tensor"),
            P("section", None, "tensor", None),
            P("section", None, "tensor", None),
            P(None, "tensor", None),
        ),
        out_specs=(P("section", None, "tensor", None), P("section", None, "tensor")),
        check_vma=False,
    )
```

profile of v0, /device:TPU:1, one launch (start us, length us, event | category | flops | bytes accessed | tf_op | source)
XLA Modules:
  0.0 854.7 jit_solution(864863359403898031)
XLA Ops:
  0.6 9.6 %copy.496 = bf16[4,4,8192]{1,0,2:T(4,128)(2,1)} copy(bf16[4,4,8192]{2,1,0:T(4,128)(2,1)} %param.31) | data formatting | bytes 524288 | tf_op args[7]
  10.2 16.8 %reshape.1614 = bf16[64,2,1024]{2,1,0:T(2,128)(2,1)} reshape(bf16[8192,4,4]{2,1,0:T(4,128)(2,1)} %bitcast.1833) | data formatting | bytes 524288
  27.1 14.6 %all-to-all-start = ((bf16[64,2,1024]{2,1,0:T(2,128)(2,1)}), bf16[64,2,1024]{2,1,0:T(2,128)(2,1)S(1)}, u32[]{:S(2)}, u32[]{:S(2)}) async-start(bf16[64,2,1024]{2,1,0:T(2,128)(2,1)} %reshape.1614), calls=%async_computation | async-start | bytes 524288 | tf_op jit(solution)/shard_map/all_to_all | solution.py:107
  43.2 6.1 broadcast_in_dim.765
  49.3 31.8 %reshape.1616 = bf16[64,2,2048]{2,1,0:T(2,128)(2,1)} reshape(bf16[16384,4,4]{2,1,0:T(4,128)(2,1)} %bitcast.1828) | data formatting | bytes 1048576
  81.1 10.6 %all-to-all-start.1 = ((bf16[64,2,2048]{2,1,0:T(2,128)(2,1)}), bf16[64,2,2048]{2,1,0:T(2,128)(2,1)S(1)}, u32[]{:S(2)}, u32[]{:S(2)}) async-start(bf16[64,2,2048]{2,1,0:T(2,128)(2,1)} %reshape.1616), calls=%async_computation.1 | async-start | bytes 1048576 | tf_op jit(solution)/shard_map/all_to_all | solution.py:56
  92.2 2.4 reduce-window.6
  95.3 2.6 copy.543
  97.9 7.2 broadcast_in_dim.766
  105.1 31.8 %reshape.1618 = bf16[64,2,2048]{2,1,0:T(2,128)(2,1)} reshape(bf16[16384,4,4]{2,1,0:T(4,128)(2,1)} %bitcast.1829) | data formatting | bytes 1048576
  138.1 11.2 %all-to-all-start.2 = ((bf16[64,2,2048]{2,1,0:T(2,128)(2,1)}), bf16[64,2,2048]{2,1,0:T(2,128)(2,1)}, u32[]{:S(2)}, u32[]{:S(2)}) async-start(bf16[64,2,2048]{2,1,0:T(2,128)(2,1)} %reshape.1618), calls=%async_computation.2 | async-start | bytes 1048576 | tf_op jit(solution)/shard_map/all_to_all | solution.py:55
  150.6 19.0 %reshape.1615 = bf16[8192,4,4]{2,1,0:T(4,128)(2,1)} reshape(bf16[64,2,1024]{2,1,0:T(2,128)(2,1)S(1)} %all-to-all-done) | data formatting | bytes 524288
  169.6 11.0 %copy.497 = bf16[4,4,64,128]{3,1,2,0:T(4,128)(2,1)S(1)} copy(bf16[4,4,64,128]{1,0,3,2:T(4,128)(2,1)} %bitcast.1832) | data formatting | bytes 524288 | tf_op jit(solution)/shard_map/all_to_all | solution.py:107
  181.3 37.0 %reshape.1617 = bf16[16384,4,4]{2,1,0:T(4,128)(2,1)} reshape(bf16[64,2,2048]{2,1,0:T(2,128)(2,1)S(1)} %all-to-all-done.1) | data formatting | bytes 1048576
  218.3 21.4 %copy.504 = bf16[4,64,4,256]{3,2,1,0:T(4,128)(2,1)S(1)} copy(bf16[4,64,4,256]{2,0,3,1:T(4,128)(2,1)} %bitcast.1830) | data formatting | bytes 1048576 | tf_op jit(solution)/shard_map/all_to_all | solution.py:56
  239.9 37.8 %reshape.1619 = bf16[16384,4,4]{2,1,0:T(4,128)(2,1)} reshape(bf16[64,2,2048]{2,1,0:T(2,128)(2,1)} %all-to-all-done.2) | data formatting | bytes 1048576
  277.7 21.8 %copy.506 = bf16[4,64,4,256]{3,2,1,0:T(4,128)(2,1)} copy(bf16[4,64,4,256]{2,0,3,1:T(4,128)(2,1)} %bitcast.1831) | data formatting | bytes 1048576 | tf_op jit(solution)/shard_map/all_to_all | solution.py:55
  300.7 1.8 conditional.8
  300.7 1.8 copy.544
  302.5 1.8 copy.510
  305.6 8.5 collective-permute-done
  315.7 2.2 conditional.9
  315.7 1.8 copy.545
  321.0 7.5 collective-permute-done.1
  330.2 1.8 conditional.10
  330.2 1.8 copy.546
  332.0 1.8 copy.516
  335.1 6.6 collective-permute-done.2
  343.4 2.0 conditional.11
  343.4 1.8 copy.547
  345.3 1.8 copy.519
  348.4 12.1 %collective-permute-done.3 = bf16[4,256,128]{2,1,0:T(8,128)(2,1)} collective-permute-done((bf16[4,256,128]{2,1,0:T(8,128)(2,1)}, bf16[4,256,128]{2,1,0:T(8,128)(2,1)}, u32[]{:S(2)}, u32[]{:S(2)}) %collective-permute-start.3) | collective-permute-done | bytes 262176 | tf_op jit(solution)/shard_map/ppermute | solution.py:21
  362.2 1.8 conditional.12
  362.2 1.8 copy.548
  364.0 1.8 copy.522
  367.1 11.3 %collective-permute-done.4 = bf16[4,256,128]{2,1,0:T(8,128)(2,1)} collective-permute-done((bf16[4,256,128]{2,1,0:T(8,128)(2,1)}, bf16[4,256,128]{2,1,0:T(8,128)(2,1)}, u32[]{:S(2)}, u32[]{:S(2)}) %collective-permute-start.4) | collective-permute-done | bytes 262176 | tf_op jit(solution)/shard_map/ppermute | solution.py:21
  380.1 2.0 conditional.13
  380.1 1.8 copy.549
  382.1 1.8 copy.525
  385.2 11.9 %collective-permute-done.5 = bf16[4,256,128]{2,1,0:T(8,128)(2,1)} collective-permute-done((bf16[4,256,128]{2,1,0:T(8,128)(2,1)}, bf16[4,256,128]{2,1,0:T(8,128)(2,1)}, u32[]{:S(2)}, u32[]{:S(2)}) %collective-permute-start.5) | collective-permute-done | bytes 262176 | tf_op jit(solution)/shard_map/ppermute | solution.py:21
  398.8 1.8 conditional.14
  398.8 1.8 copy.550
  400.6 1.8 copy.528
  403.7 369.7 %collective-permute-done.6 = bf16[4,256,128]{2,1,0:T(8,128)(2,1)} collective-permute-done((bf16[4,256,128]{2,1,0:T(8,128)(2,1)}, bf16[4,256,128]{2,1,0:T(8,128)(2,1)}, u32[]{:S(2)}, u32[]{:S(2)}) %collective-permute-start.6) | collective-permute-done | bytes 262176 | tf_op jit(solution)/shard_map/ppermute | solution.py:21
  775.0 38.0 %conditional.15 = (bf16[4,256,128]{1,2,0:T(8,128)(2,1)S(1)}, f32[4,128]{1,0:T(4,128)S(1)}) conditional(s32[]{:T(128)} %convert_element_type.1020, (bf16[4,256,128]{2,1,0:T(8,128)(2,1)}) %tuple.104, (bf16[4,256,128]{2,1,0:T(8,128)(2,1)}, f32[4,128]{1,0:T(4,128)S(1)}, pred[256,256]{1,0:T(8,128)(4,1)}, pred[256,256]{1,0:T(8,128)(4,1)}, ...), branch_computations={%region_128.129_spmd, %region_129.146_spmd} | conditional | flops 327263744 | bytes 15730360 | solution.py:133
  782.1 2.0 convolution_bitcast_fusion.58
  816.0 24.9 %all-to-all-start.3 = ((bf16[4,256,128]{2,0,1:T(4,128)(2,1)}), bf16[4,256,128]{2,0,1:T(4,128)(2,1)S(1)}, u32[]{:S(2)}, u32[]{:S(2)}) async-start(bf16[4,256,128]{2,0,1:T(4,128)(2,1)} %copy.539), calls=%async_computation.3 | async-start | bytes 524288 | tf_op jit(solution)/shard_map/all_to_all | solution.py:138
  841.5 11.9 %all-to-all-done.3 = bf16[4,256,128]{2,0,1:T(4,128)(2,1)S(1)} async-done(((bf16[4,256,128]{2,0,1:T(4,128)(2,1)}), bf16[4,256,128]{2,0,1:T(4,128)(2,1)S(1)}, u32[]{:S(2)}, u32[]{:S(2)}) %all-to-all-start.3) | async-done | bytes 262176 | tf_op jit(solution)/shard_map/all_to_all | solution.py:138
  (130 shorter events, 69.6 us)
Async XLA Ops:
  0.6 41.0 %copy-start.31 = (bf16[1,4,4,2048]{3,2,1,0:T(4,128)(2,1)S(1)}, bf16[1,4,4,2048]{3,2,1,0:T(4,128)(2,1)}, u32[]{:S(2)}) copy-start(bf16[1,4,4,2048]{3,2,1,0:T(4,128)(2,1)} %param.30) | copy-start | bytes 196612
  27.1 54.0 %all-to-all-start = ((bf16[64,2,1024]{2,1,0:T(2,128)(2,1)}), bf16[64,2,1024]{2,1,0:T(2,128)(2,1)S(1)}, u32[]{:S(2)}, u32[]{:S(2)}) async-start(bf16[64,2,1024]{2,1,0:T(2,128)(2,1)} %reshape.1614), calls=%async_computation | async-start | bytes 524288 | tf_op jit(solution)/shard_map/all_to_all | solution.py:107
  43.1 48.6 %copy-start.33 = (f32[1,1024,2]{1,2,0:T(2,128)S(1)}, f32[1,1024,2]{1,2,0:T(2,128)}, u32[]{:S(2)}) copy-start(f32[1,1024,2]{1,2,0:T(2,128)} %param.26) | copy-start | bytes 24580
  43.2 48.8 %copy-start.44 = (f32[1,2]{1,0:T(1,128)S(1)}, f32[1,2]{1,0:T(1,128)}, u32[]{:S(2)}) copy-start(f32[1,2]{1,0:T(1,128)} %param.27) | copy-start | bytes 28
  43.2 52.1 %copy-start.32 = (bf16[1,4,4,2048]{3,2,1,0:T(4,128)(2,1)S(1)}, bf16[1,4,4,2048]{3,2,1,0:T(4,128)(2,1)}, u32[]{:S(2)}) copy-start(bf16[1,4,4,2048]{3,2,1,0:T(4,128)(2,1)} %param.29) | copy-start | bytes 196612
  81.1 57.0 %all-to-all-start.1 = ((bf16[64,2,2048]{2,1,0:T(2,128)(2,1)}), bf16[64,2,2048]{2,1,0:T(2,128)(2,1)S(1)}, u32[]{:S(2)}, u32[]{:S(2)}) async-start(bf16[64,2,2048]{2,1,0:T(2,128)(2,1)} %reshape.1616), calls=%async_computation.1 | async-start | bytes 1048576 | tf_op jit(solution)/shard_map/all_to_all | solution.py:56
  97.9 39.0 %copy-start.30 = (bf16[1,1024,128]{2,1,0:T(8,128)(2,1)S(1)}, bf16[1,1024,128]{2,1,0:T(8,128)(2,1)}, u32[]{:S(2)}) copy-start(bf16[1,1024,128]{2,1,0:T(8,128)(2,1)} %param.24) | copy-start | bytes 786436
  97.9 52.1 %copy-start.43 = (bf16[1,4,128]{2,1,0:T(4,128)(2,1)S(1)}, bf16[1,4,128]{2,1,0:T(4,128)(2,1)}, u32[]{:S(2)}) copy-start(bf16[1,4,128]{2,1,0:T(4,128)(2,1)} %param.25) | copy-start | bytes 3076
  138.1 101.7 %all-to-all-start.2 = ((bf16[64,2,2048]{2,1,0:T(2,128)(2,1)}), bf16[64,2,2048]{2,1,0:T(2,128)(2,1)}, u32[]{:S(2)}, u32[]{:S(2)}) async-start(bf16[64,2,2048]{2,1,0:T(2,128)(2,1)} %reshape.1618), calls=%async_computation.2 | async-start | bytes 1048576 | tf_op jit(solution)/shard_map/all_to_all | solution.py:55
  239.8 60.8 %copy-start.29 = (f32[1,2]{1,0:T(1,128)S(1)}, f32[1,2]{1,0:T(1,128)}, u32[]{:S(2)}) copy-start(f32[1,2]{1,0:T(1,128)} %param.28) | copy-start | bytes 28
  302.5 13.2 %copy-start.34 = (f32[4,128]{1,0:T(4,128)}, f32[4,128]{1,0:T(4,128)S(1)}, u32[]{:S(2)}) copy-start(f32[4,128]{1,0:T(4,128)S(1)} %get-tuple-element.417) | copy-start | bytes 6148
  304.3 9.7 %collective-permute-start = (bf16[4,256,128]{2,1,0:T(8,128)(2,1)}, bf16[4,256,128]{2,1,0:T(8,128)(2,1)}, u32[]{:S(2)}, u32[]{:S(2)}) collective-permute-start(bf16[4,256,128]{2,1,0:T(8,128)(2,1)} %copy.510), channel_id=1, source_target_pairs={{64,0},{128,64},{192,128},{256,192},{320,256},{384,320},{448,384},... | collective-permute-start | bytes 786440 | tf_op jit(solution)/shard_map/ppermute | solution.py:21
  317.9 12.3 %copy-start.36 = (f32[4,128]{1,0:T(4,128)}, f32[4,128]{1,0:T(4,128)S(1)}, u32[]{:S(2)}) copy-start(f32[4,128]{1,0:T(4,128)S(1)} %get-tuple-element.416) | copy-start | bytes 6148
  319.7 8.8 %collective-permute-start.1 = (bf16[4,256,128]{2,1,0:T(8,128)(2,1)}, bf16[4,256,128]{2,1,0:T(8,128)(2,1)}, u32[]{:S(2)}, u32[]{:S(2)}) collective-permute-start(bf16[4,256,128]{2,1,0:T(8,128)(2,1)} %copy.513), channel_id=1, source_target_pairs={{64,0},{128,64},{192,128},{256,192},{320,256},{384,320},{448,384},... | collective-permute-start | bytes 786440 | tf_op jit(solution)/shard_map/ppermute | solution.py:21
  332.0 11.4 %copy-start.38 = (f32[4,128]{1,0:T(4,128)}, f32[4,128]{1,0:T(4,128)S(1)}, u32[]{:S(2)}) copy-start(f32[4,128]{1,0:T(4,128)S(1)} %get-tuple-element.415) | copy-start | bytes 6148
  333.8 7.9 collective-permute-start.2
  345.3 16.9 %copy-start.39 = (f32[4,128]{1,0:T(4,128)}, f32[4,128]{1,0:T(4,128)S(1)}, u32[]{:S(2)}) copy-start(f32[4,128]{1,0:T(4,128)S(1)} %get-tuple-element.414) | copy-start | bytes 6148
  347.1 13.4 %collective-permute-start.3 = (bf16[4,256,128]{2,1,0:T(8,128)(2,1)}, bf16[4,256,128]{2,1,0:T(8,128)(2,1)}, u32[]{:S(2)}, u32[]{:S(2)}) collective-permute-start(bf16[4,256,128]{2,1,0:T(8,128)(2,1)} %copy.519), channel_id=1, source_target_pairs={{64,0},{128,64},{192,128},{256,192},{320,256},{384,320},{448,384},... | collective-permute-start | bytes 786440 | tf_op jit(solution)/shard_map/ppermute | solution.py:21
  364.0 16.1 %copy-start.40 = (f32[4,128]{1,0:T(4,128)}, f32[4,128]{1,0:T(4,128)S(1)}, u32[]{:S(2)}) copy-start(f32[4,128]{1,0:T(4,128)S(1)} %get-tuple-element.413) | copy-start | bytes 6148
  365.8 12.6 %collective-permute-start.4 = (bf16[4,256,128]{2,1,0:T(8,128)(2,1)}, bf16[4,256,128]{2,1,0:T(8,128)(2,1)}, u32[]{:S(2)}, u32[]{:S(2)}) collective-permute-start(bf16[4,256,128]{2,1,0:T(8,128)(2,1)} %copy.522), channel_id=1, source_target_pairs={{64,0},{128,64},{192,128},{256,192},{320,256},{384,320},{448,384},... | collective-permute-start | bytes 786440 | tf_op jit(solution)/shard_map/ppermute | solution.py:21
  382.1 16.7 %copy-start.41 = (f32[4,128]{1,0:T(4,128)}, f32[4,128]{1,0:T(4,128)S(1)}, u32[]{:S(2)}) copy-start(f32[4,128]{1,0:T(4,128)S(1)} %get-tuple-element.412) | copy-start | bytes 6148
  383.9 13.2 %collective-permute-start.5 = (bf16[4,256,128]{2,1,0:T(8,128)(2,1)}, bf16[4,256,128]{2,1,0:T(8,128)(2,1)}, u32[]{:S(2)}, u32[]{:S(2)}) collective-permute-start(bf16[4,256,128]{2,1,0:T(8,128)(2,1)} %copy.525), channel_id=1, source_target_pairs={{64,0},{128,64},{192,128},{256,192},{320,256},{384,320},{448,384},... | collective-permute-start | bytes 786440 | tf_op jit(solution)/shard_map/ppermute | solution.py:21
  400.5 374.5 %copy-start.42 = (f32[4,128]{1,0:T(4,128)}, f32[4,128]{1,0:T(4,128)S(1)}, u32[]{:S(2)}) copy-start(f32[4,128]{1,0:T(4,128)S(1)} %get-tuple-element.411) | copy-start | bytes 6148
  400.5 440.3 %copy-start.35 = (f32[4,128]{1,0:T(4,128)S(1)}, f32[4,128]{1,0:T(4,128)}, u32[]{:S(2)}) copy-start(f32[4,128]{1,0:T(4,128)} %copy-done.34) | copy-start | bytes 6148
  400.6 440.3 %copy-start.37 = (f32[4,128]{1,0:T(4,128)S(1)}, f32[4,128]{1,0:T(4,128)}, u32[]{:S(2)}) copy-start(f32[4,128]{1,0:T(4,128)} %copy-done.36) | copy-start | bytes 6148
  402.4 371.0 %collective-permute-start.6 = (bf16[4,256,128]{2,1,0:T(8,128)(2,1)}, bf16[4,256,128]{2,1,0:T(8,128)(2,1)}, u32[]{:S(2)}, u32[]{:S(2)}) collective-permute-start(bf16[4,256,128]{2,1,0:T(8,128)(2,1)} %copy.528), channel_id=1, source_target_pairs={{64,0},{128,64},{192,128},{256,192},{320,256},{384,320},{448,384},... | collective-permute-start | bytes 786440 | tf_op jit(solution)/shard_map/ppermute | solution.py:21
  813.1 0.7 copy-start.7
  816.0 37.5 %all-to-all-start.3 = ((bf16[4,256,128]{2,0,1:T(4,128)(2,1)}), bf16[4,256,128]{2,0,1:T(4,128)(2,1)S(1)}, u32[]{:S(2)}, u32[]{:S(2)}) async-start(bf16[4,256,128]{2,0,1:T(4,128)(2,1)} %copy.539), calls=%async_computation.3 | async-start | bytes 524288 | tf_op jit(solution)/shard_map/all_to_all | solution.py:138
where the time goes:
time: 867 us; the launch traced here: 855 us
  waiting for transfers between devices  439 us (51%)
  local copies, waits for them, and re-layouts  306 us (35%)
  starting transfers between devices  70.2 us (8%)
  other arithmetic  22.6 us (3%)
  matrix products  13.6 us (2%)
    ppermute x7, waiting for transfers between devices, passed_along(): return lax.ppermute(array, axis, pairs)  428 us
    unnamed x43, local copies, waits for them, and re-layouts  185 us
    all_to_all x1, starting transfers between devices, on_device(): lax.all_to_all(as_sent(stream_heads), 'tensor', split_axis=1, concat_axis...  24.9 us
    all_to_all x2, local copies, waits for them, and re-layouts, on_device(): lax.all_to_all(widen_groups(b_matrix), 'tensor', split_axis=2, concat_axi...  23 us
    all_to_all x2, local copies, waits for them, and re-layouts, on_device(): lax.all_to_all(widen_groups(c_matrix), 'tensor', split_axis=2, concat_axi...  21.5 us
  transfers between devices with their start and end apart: 11, of which 8 were waited for; matrix products, arithmetic and copies ran while one was open for 21% of the time, Pallas kernels for 0%

commit v1 on v0

v1 whole, which is shorter than its diff:
```python
import functools

import jax
import jax.numpy as jnp
from jax import lax
from jax.experimental import pallas as pl
from jax.experimental.pallas import tpu as pltpu
from jax.sharding import PartitionSpec as P

P_SIZE = 64
N = 256
K = 4
BLOCKS = 4
CHUNK = 128
PAD = 8
F32 = jnp.float32
BF16 = jnp.bfloat16


def dot(a, b):
    return jnp.dot(a, b, preferred_element_type=F32)


def kernel(
    sizes,
    act_ref,
    taps_ref,
    step_ref,
    rate_ref,
    skip_ref,
    b_ref,
    c_ref,
    top_ref,
    out_ref,
    conv_ref,
    staged,
    bc_send,
    bc_rows,
    bc_all,
    top_send,
    top_rows,
    top_all,
    act_pad,
    slope,
    grow,
    shrink,
    b_flat,
    c_flat,
    scores,
    carried,
    dy,
    stream,
    extended,
    out_send,
    out_rows,
    out_all,
    bc1_s,
    bc1_r,
    bc2_s,
    bc2_r,
    bc3_s,
    bc3_r,
    top1_s,
    top1_r,
    top2_s,
    top2_r,
    hop_s,
    hop_r,
    out1_s,
    out1_r,
    out2_s,
    out2_r,
    local_s,
):
    sections, ys, ws, chunk = sizes
    block = 4 * ys * ws
    length = BLOCKS * block
    chunks = length // chunk
    zs = ws // 2
    run = 4 * ws
    sec = lax.axis_index("section")
    pos = lax.axis_index("tensor")
    y = pos // ws
    w = pos % ws
    z = w // 2
    core = w % 2
    top_layer = sec == sections - 1

    def remote(src, dst, send, recv, section, tensor):
        return pltpu.make_async_remote_copy(
            src_ref=src,
            dst_ref=dst,
            send_sem=send,
            recv_sem=recv,
            device_id=(section, tensor),
            device_id_type=pl.DeviceIdType.MESH,
        )

    def other_y(d):
        return lax.rem(y + d, ys) * ws + w

    def other_w(d):
        return y * ws + lax.rem(w + d, ws)

    def other_z(d):
        return y * ws + lax.rem(z + d, zs) * 2 + core

    sibling = y * ws + z * 2 + (1 - core)

    barrier = pltpu.get_barrier_semaphore()

    def greet(section, tensor):
        pl.semaphore_signal(
            barrier, inc=1, device_id=(section, tensor), device_id_type=pl.DeviceIdType.MESH
        )

    for d in range(1, ys):
        greet(sec, other_y(d))
    for d in range(1, ws):
        greet(sec, other_w(d))

    greet(lax.rem(sec + sections - 1, sections), pos)
    greet(lax.rem(sec + 1, sections), pos)

    for at in range(BLOCKS):
        staged[4 * at : 4 * at + 4, 0 : ys * N] = b_ref[at].astype(F32)
        staged[4 * at : 4 * at + 4, ys * N : 2 * ys * N] = c_ref[at].astype(F32)
    for g in range(ys):
        bc_send[g, :, 0:N] = staged[:, g * N : (g + 1) * N].astype(BF16)
        bc_send[g, :, N : 2 * N] = staged[:, (ys + g) * N : (ys + g + 1) * N].astype(BF16)

    pl.semaphore_wait(barrier, ys + ws)

    def bc1(d):
        return remote(
            bc_send.at[lax.rem(y + d, ys)], bc_rows.at[y], bc1_s.at[d], bc1_r.at[d], sec, other_y(d)
        )

    def bc1_in(d):
        at = lax.rem(y + ys - d, ys)
        return remote(bc_send.at[at], bc_rows.at[at], bc1_s.at[d], bc1_r.at[d], sec, other_y(d))

    for d in range(1, ys):
        bc1(d).start()
    bc_rows[pl.ds(y, 1)] = bc_send[pl.ds(y, 1)]

    def top1(d):
        return remote(
            top_send.at[lax.rem(y + d, ys)],
            top_rows.at[y],
            top1_s.at[d],
            top1_r.at[d],
            sec,
            other_y(d),
        )

    def top1_in(d):
        at = lax.rem(y + ys - d, ys)
        return remote(top_send.at[at], top_rows.at[at], top1_s.at[d], top1_r.at[d], sec, other_y(d))

    wide = ws * 2 * P_SIZE

    @pl.when(top_layer)
    def _():
        for at in range(BLOCKS):
            staged[4 * at : 4 * at + 4, :] = top_ref[at].astype(F32)
        for g in range(ys):
            top_send[g] = staged[:, g * wide : (g + 1) * wide].astype(BF16)
        for d in range(1, ys):
            top1(d).start()
        top_rows[pl.ds(y, 1)] = top_send[pl.ds(y, 1)]

    act_pad[0:PAD, :] = jnp.zeros((PAD, 2 * P_SIZE), F32)
    act_pad[PAD:, :] = act_ref[...].astype(F32)
    taps = taps_ref[...].astype(F32)
    first = lax.broadcasted_iota(jnp.int32, (1, 2 * P_SIZE), 1) < P_SIZE
    rate = jnp.where(first, rate_ref[:, 0:1], rate_ref[:, 1:2])
    skip = jnp.where(first, skip_ref[:, 0:1], skip_ref[:, 1:2])
    row_at = lax.broadcasted_iota(jnp.int32, (chunk, chunk), 0)
    col_at = lax.broadcasted_iota(jnp.int32, (chunk, chunk), 1)
    lower = (row_at >= col_at).astype(F32).astype(BF16)
    for at in range(chunks):
        rows = slice(at * chunk, (at + 1) * chunk)
        preact = jnp.zeros((chunk, 2 * P_SIZE), F32)
        for k in range(K):
            start = PAD + at * chunk - k
            preact = preact + taps[k : k + 1] * act_pad[start : start + chunk, :]
        logistic = 1.0 / (1.0 + jnp.exp(-preact))
        slope[rows, :] = logistic * (1.0 + preact * (1.0 - logistic))
        step = jnp.concatenate(
            [jnp.broadcast_to(step_ref[h : h + 1, rows], (P_SIZE, chunk)) for h in range(2)], axis=0
        ).T
        high = step.astype(BF16)
        rest = step - high.astype(F32)
        mid = rest.astype(BF16)
        low = (rest - mid.astype(F32)).astype(BF16)
        decay = -rate * (dot(lower, high) + dot(lower, mid) + dot(lower, low))
        grow[rows, :] = jnp.exp(decay)
        shrink[rows, :] = step * jnp.exp(-decay)
    carried[...] = jnp.zeros_like(carried)
    extended[length:, :] = jnp.zeros((PAD, 2 * P_SIZE), F32)

    side = 16 * ws
    out_at = lax.broadcasted_iota(jnp.int32, (side, side), 0)
    in_at = lax.broadcasted_iota(jnp.int32, (side, side), 1)

    def source_of(at):
        return ((at // 4) % ws) * 16 + (at // run) * 4 + at % 4

    gather = (source_of(out_at) == in_at).astype(F32).astype(BF16)
    scatter = (source_of(in_at) == out_at).astype(F32).astype(BF16)

    def part(of):
        return bc_all.at[:, pl.ds(pl.multiple_of(of * 16, 16), 16), :]

    def bc2(d):
        to = sibling if d == 0 else other_z(d)
        return remote(bc_rows, part(w), bc2_s.at[d], bc2_r.at[d], sec, to)

    def bc2_in(d):
        of = z * 2 + (1 - core) if d == 0 else lax.rem(z + zs - d, zs) * 2 + core
        return remote(bc_rows, part(of), bc2_s.at[d], bc2_r.at[d], sec, sibling)

    def bc3(d):
        of = lax.rem(z + zs - d, zs) * 2 + core
        return remote(part(of), part(of), bc3_s.at[d], bc3_r.at[d], sec, sibling)

    def bc3_in(d):
        of = lax.rem(z + zs - d, zs) * 2 + (1 - core)
        return remote(part(of), part(of), bc3_s.at[d], bc3_r.at[d], sec, sibling)

    for d in range(1, ys):
        bc1_in(d).wait_recv()
    for d in list(range(zs - 1, 0, -1)) + [0]:
        bc2(d).start()
    own = pltpu.make_async_copy(bc_rows, part(w), local_s.at[0])
    own.start()

    def columns(of):
        return pl.ds(pl.multiple_of(of * 2 * P_SIZE, 2 * P_SIZE), 2 * P_SIZE)

    def slab(of):
        return pl.ds(pl.multiple_of(of * 16, 16), 16)

    def top2(d):
        to = lax.rem(w + d, ws)
        return remote(
            top_rows.at[:, :, columns(to)],
            top_all.at[:, slab(w), :],
            top2_s.at[d],
            top2_r.at[d],
            sec,
            other_w(d),
        )

    def top2_in(d):
        of = lax.rem(w + ws - d, ws)
        return remote(
            top_rows.at[:, :, columns(of)],
            top_all.at[:, slab(of), :],
            top2_s.at[d],
            top2_r.at[d],
            sec,
            other_w(d),
        )

    @pl.when(top_layer)
    def _():
        for d in range(1, ys):
            top1_in(d).wait_recv()
        for d in range(1, ws):
            top2(d).start()
        mine = pltpu.make_async_copy(
            top_rows.at[:, :, columns(w)], top_all.at[:, slab(w), :], local_s.at[1]
        )
        mine.start()
        mine.wait()

    for d in range(1, zs):
        bc2_in(d).wait_recv()
        bc3(d).start()
    own.wait()
    bc2_in(0).wait_recv()
    for d in range(1, zs):
        bc3_in(d).wait_recv()

    for g in range(ys):
        both = dot(gather, bc_all[g]).astype(BF16)
        for at in range(BLOCKS):
            start = at * block + g * run
            b_flat[start : start + run, :] = both[at * run : (at + 1) * run, 0:N]
            c_flat[start : start + run, :] = both[at * run : (at + 1) * run, N : 2 * N]

    for at in range(chunks):
        rows = slice(at * chunk, (at + 1) * chunk)
        product = lax.dot_general(
            b_flat[rows, :], c_flat[rows, :], (((1,), (1,)), ((), ())), preferred_element_type=F32
        )
        scores[rows, :] = jnp.where(col_at >= row_at, product, 0.0).astype(BF16)

    @pl.when(top_layer)
    def _():
        for d in range(1, ws):
            top2_in(d).wait_recv()
        for g in range(ys):
            ordered = dot(gather, top_all[g]).astype(BF16)
            for at in range(BLOCKS):
                start = at * block + g * run
                dy[start : start + run, :] = ordered[at * run : (at + 1) * run, :]

    def hop(at):
        rows = pl.ds(at * chunk, chunk)
        return remote(
            stream.at[rows, :],
            dy.at[rows, :],
            hop_s.at[at],
            hop_r.at[at],
            lax.rem(sec + sections - 1, sections),
            pos,
        )

    conv = [jnp.zeros((1, 2 * P_SIZE), F32) for _ in range(K)]
    for at in range(chunks - 1, -1, -1):
        rows = slice(at * chunk, (at + 1) * chunk)

        @pl.when(jnp.logical_not(top_layer))
        def _():
            hop(at).wait_recv()

        upstream = dy[rows, :].astype(F32)
        fed = (grow[rows, :] * upstream).astype(BF16)
        ended = grow[(at + 1) * chunk - 1 : (at + 1) * chunk, :] * carried[...]
        mixed = dot(scores[rows, :], fed) + dot(b_flat[rows, :], ended.astype(BF16))
        grad_pre = (shrink[rows, :] * mixed + skip * upstream) * slope[rows, :]
        extended[rows, :] = grad_pre
        grad_in = taps[0:1] * grad_pre
        for k in range(1, K):
            start = at * chunk + k
            grad_in = grad_in + taps[k : k + 1] * extended[start : start + chunk, :]
        stream[rows, :] = (upstream + grad_in.astype(BF16).astype(F32)).astype(BF16)

        @pl.when(sec > 0)
        def _():
            hop(at).start()

        carried[...] = ended + lax.dot_general(
            c_flat[rows, :], fed, (((0,), (0,)), ((), ())), preferred_element_type=F32
        )
        for k in range(K):
            start = PAD + at * chunk - k
            conv[k] = conv[k] + jnp.sum(
                grad_pre * act_pad[start : start + chunk, :], axis=0, keepdims=True
            )
    for k in range(K):
        conv_ref[k : k + 1, :] = conv[k]

    for g in range(ys):
        natural = jnp.concatenate(
            [stream[at * block + g * run : at * block + (g + 1) * run, :] for at in range(BLOCKS)],
            axis=0,
        )
        ordered = dot(scatter, natural).astype(BF16)
        for v in range(ws):
            out_send[v, g] = ordered[v * 16 : (v + 1) * 16, :]

    def out1(d):
        return remote(
            out_send.at[lax.rem(w + d, ws)],
            out_rows.at[:, :, columns(w)],
            out1_s.at[d],
            out1_r.at[d],
            sec,
            other_w(d),
        )

    def out1_in(d):
        of = lax.rem(w + ws - d, ws)
        return remote(
            out_send.at[of],
            out_rows.at[:, :, columns(of)],
            out1_s.at[d],
            out1_r.at[d],
            sec,
            other_w(d),
        )

    def wide_columns(of):
        return pl.ds(pl.multiple_of(of * wide, wide), wide)

    def out2(d):
        return remote(
            out_rows.at[lax.rem(y + d, ys)],
            out_all.at[:, wide_columns(y)],
            out2_s.at[d],
            out2_r.at[d],
            sec,
            other_y(d),
        )

    def out2_in(d):
        of = lax.rem(y + ys - d, ys)
        return remote(
            out_rows.at[of],
            out_all.at[:, wide_columns(of)],
            out2_s.at[d],
            out2_r.at[d],
            sec,
            other_y(d),
        )

    for d in range(1, ws):
        out1(d).start()
    kept = pltpu.make_async_copy(out_send.at[w], out_rows.at[:, :, columns(w)], local_s.at[2])
    kept.start()
    kept.wait()
    for d in range(1, ws):
        out1_in(d).wait_recv()
    for d in range(1, ys):
        out2(d).start()
    last = pltpu.make_async_copy(out_rows.at[y], out_all.at[:, wide_columns(y)], local_s.at[3])
    last.start()
    last.wait()

    for d in range(1, ys):
        bc1(d).wait_send()
    for d in range(zs):
        bc2(d).wait_send()
    for d in range(1, zs):
        bc3(d).wait_send()

    @pl.when(top_layer)
    def _():
        for d in range(1, ys):
            top1(d).wait_send()
        for d in range(1, ws):
            top2(d).wait_send()

    @pl.when(sec > 0)
    def _():
        for at in range(chunks):
            hop(at).wait_send()

    for d in range(1, ws):
        out1(d).wait_send()
    for d in range(1, ys):
        out2_in(d).wait_recv()
    staged[...] = out_all[...].astype(F32)
    for at in range(BLOCKS):
        out_ref[at] = staged[4 * at : 4 * at + 4, :].astype(BF16)
    for d in range(1, ys):
        out2(d).wait_send()


def on_device(
    activations, conv_weight, step_size, decay_rate, skip_gain, b_matrix, c_matrix, top_grad
):
    tensor_size = lax.axis_size("tensor")
    sections = lax.axis_size("section")
    ys = b_matrix.shape[-1] // N
    ws = tensor_size // ys
    length, width = activations.shape[1:]
    chunk = min(CHUNK, length // BLOCKS)
    chunks = length // chunk
    zs = ws // 2
    dma = pltpu.SemaphoreType.DMA
    out, conv = pl.pallas_call(
        functools.partial(kernel, (sections, ys, ws, chunk)),
        out_shape=(
            jax.ShapeDtypeStruct(top_grad.shape, BF16),
            jax.ShapeDtypeStruct((K, width), F32),
        ),
        in_specs=[pl.BlockSpec(memory_space=pltpu.VMEM)] * 8,
        out_specs=(pl.BlockSpec(memory_space=pltpu.VMEM),) * 2,
        scratch_shapes=[
            pltpu.VMEM((16, top_grad.shape[-1]), F32),
            pltpu.VMEM((ys, 16, 2 * N), BF16),
            pltpu.VMEM((ys, 16, 2 * N), BF16),
            pltpu.VMEM((ys, 16 * ws, 2 * N), BF16),
            pltpu.VMEM((ys, 16, ws * width), BF16),
            pltpu.VMEM((ys, 16, ws * width), BF16),
            pltpu.VMEM((ys, 16 * ws, width), BF16),
            pltpu.VMEM((PAD + length, width), F32),
            pltpu.VMEM((length, width), F32),
            pltpu.VMEM((length, width), F32),
            pltpu.VMEM((length, width), F32),
            pltpu.VMEM((length, N), BF16),
            pltpu.VMEM((length, N), BF16),
            pltpu.VMEM((length, chunk), BF16),
            pltpu.VMEM((N, width), F32),
            pltpu.VMEM((length, width), BF16),
            pltpu.VMEM((length, width), BF16),
            pltpu.VMEM((length + PAD, width), F32),
            pltpu.VMEM((ws, ys, 16, width), BF16),
            pltpu.VMEM((ys, 16, ws * width), BF16),
            pltpu.VMEM((16, ys * ws * width), BF16),
            dma((ys,)),
            dma((ys,)),
            dma((zs,)),
            dma((zs,)),
            dma((zs,)),
            dma((zs,)),
            dma((ys,)),
            dma((ys,)),
            dma((ws,)),
            dma((ws,)),
            dma((chunks,)),
            dma((chunks,)),
            dma((ws,)),
            dma((ws,)),
            dma((ys,)),
            dma((ys,)),
            dma((4,)),
        ],
        compiler_params=pltpu.CompilerParams(
            collective_id=0, has_side_effects=True, vmem_limit_bytes=40 * 1024 * 1024
        ),
    )(
        activations[0],
        conv_weight[0],
        step_size[0].T,
        decay_rate,
        skip_gain,
        b_matrix[0],
        c_matrix[0],
        top_grad,
    )
    return (out[None], conv[None])


def solution(mesh):
    return jax.shard_map(
        on_device,
        mesh=mesh,
        in_specs=(
            P("section", None, "tensor"),
            P("section", None, "tensor"),
            P("section", None, "tensor"),
            P("section", "tensor"),
            P("section", "tensor"),
            P("section", None, "tensor", None),
            P("section", None, "tensor", None),
            P(None, "tensor", None),
        ),
        out_specs=(P("section", None, "tensor", None), P("section", None, "tensor")),
        check_vma=False,
    )
```

time: 867 us -> 96.8 us (0.11); the launches traced: 855 us -> 96.1 us
  waiting for transfers between devices: 439 us -> 0 us
  local copies, waits for them, and re-layouts: 306 us -> 6.85 us
  Pallas kernels: 0 us -> 88.6 us
  starting transfers between devices: 70.2 us -> 0 us
  other arithmetic: 22.6 us -> 0 us
  matrix products: 13.6 us -> 0 us
    ppermute x7 -> x0, waiting for transfers between devices: 428 us -> none  [passed_along(): return lax.ppermute(array, axis, pairs)]
    unnamed x43 -> x18, local copies, waits for them, and re-layouts: 185 us -> 6.85 us
    pallas_call x0 -> x1, Pallas kernels: none -> 88.6 us  [on_device(): pl.pallas_call(functools.partial(kernel, (sections, ys, ws, chunk)), out_...]
    all_to_all x4 -> x0, starting transfers between devices: 61.3 us -> none  [the longest x1 24.9 us: on_device(): lax.all_to_all(as_sent(stream_heads), 'tensor', split_axis=1, concat_axis...]
    all_to_all x6 -> x0, local copies, waits for them, and re-layouts: 56.2 us -> none  [the longest x2 23 us: on_device(): lax.all_to_all(widen_groups(b_matrix), 'tensor', split_axis=2, concat_axi...]
    cond x8 -> x0, local copies, waits for them, and re-layouts: 13.7 us -> none  [on_device(): lax.cond(active, whole_layer, pass_through, upstream)]
    dot_general x14 -> x0, matrix products: 13.6 us -> none  [the longest x4 5.77 us: block_back(): jnp.einsum('hji,jhp->ihp', weight, grad_heads, preferred_element_type=jnp...]
    select_n x8 -> x0, local copies, waits for them, and re-layouts: 13.5 us -> none  [the longest x7 12.6 us: on_device(): upstream = jnp.where(section_pos == section_count - 1, grad_top, received)]
  transfers between devices with their start and end apart: 11 -> 0, of which waited for: 8 -> 0; matrix products, arithmetic and copies ran while one was open for 21% -> 0% of each run, Pallas kernels for 0% -> 0%
where the time goes in v1:
time: 96.8 us; the launch traced here: 96.1 us
  Pallas kernels  88.6 us (92%)
  local copies, waits for them, and re-layouts  6.85 us (7%)
    pallas_call x1, Pallas kernels, on_device(): pl.pallas_call(functools.partial(kernel, (sections, ys, ws, chunk)), out_...  88.6 us
    unnamed x18, local copies, waits for them, and re-layouts  6.85 us

profile of v1, /device:TPU:1, one launch (start us, length us, event | category | flops | bytes accessed | tf_op | source)
XLA Modules:
  0.0 96.1 jit_solution(10278450679589219434)
XLA Ops:
  0.6 0.0 copy-start.4
  0.6 0.0 copy-start.5
  0.7 0.7 copy-done.4
  1.3 0.0 copy-done.5
  1.3 0.0 copy-start
  1.3 0.9 copy-done
  2.3 0.0 copy-start.1
  2.3 0.9 copy-done.1
  3.2 0.0 copy-start.2
  3.2 0.8 copy-done.2
  4.1 0.0 copy-start.3
  4.1 0.8 copy-done.3
  4.9 0.0 copy-start.6
  4.9 0.7 copy-done.6
  5.6 0.0 copy-start.7
  5.6 0.7 copy-done.7
  6.2 88.6 %shard_map.95 = (bf16[4,4,8192]{2,1,0:T(4,128)(2,1)S(1)}, f32[4,128]{1,0:T(4,128)S(1)}) custom-call(bf16[1024,128]{1,0:T(8,128)(2,1)S(1)} %bitcast.10, bf16[4,128]{1,0:T(4,128)(2,1)S(1)} %bitcast.15, f32[2,1024]{1,0:T(2,128)S(1)} %bitcast.13, f32[1,2]{1,0:T(1,128)S(1)} %copy-done.6, f32[1,2]{1,0:T(1,128)S(1)} %copy-done.7, bf16[4,4,2048]{2,1,0:T(4,128)(2,1)S(1)} %bitcast.11, ...), custom_call_target="tpu_custom_call" | custom-call | tf_op jit(solution)/shard_map/pallas_call | solution.py:466
  94.8 0.7 copy.12
  95.5 0.6 copy.13
Async XLA Ops:
  0.6 0.7 copy-start.4
  0.6 0.7 copy-start.5
  1.3 1.0 copy-start
  2.3 0.9 copy-start.1
  3.2 0.8 copy-start.2
  4.1 0.8 copy-start.3
  4.9 0.7 copy-start.6
  5.6 0.7 copy-start.7

commit v2 on v0

v2 whole, which is shorter than its diff:
```python
import functools

import jax
import jax.numpy as jnp
from jax import lax
from jax.experimental import pallas as pl
from jax.experimental.pallas import tpu as pltpu
from jax.sharding import PartitionSpec as P

P_SIZE = 64
N = 256
K = 4
BLOCKS = 4
CHUNK = 128
HALVES = 2
EARLY = 3
LAG = 3
PACED = 6
PAD = 8
F32 = jnp.float32
BF16 = jnp.bfloat16


def dot(a, b):
    return jnp.dot(a, b, preferred_element_type=F32)


def kernel(
    sizes,
    act_ref,
    taps_ref,
    step_ref,
    rate_ref,
    skip_ref,
    b_ref,
    c_ref,
    top_ref,
    out_ref,
    conv_ref,
    act_in,
    taps_in,
    step_in,
    rate_in,
    skip_in,
    bc_rows,
    bc_all,
    top_rows,
    top_all,
    top_block,
    act_pad,
    slope,
    grow,
    shrink,
    b_flat,
    c_turned,
    scores,
    carried,
    dy,
    stream,
    extended,
    out_send,
    out_rows,
    in_sem,
    bc1_s,
    bc1_r,
    bc2_s,
    bc2_r,
    bc3_r,
    top_s,
    top1_r,
    top2_r,
    hop_s,
    hop_r,
    out1_s,
    out1_r,
    out2_s,
    out2_r,
):
    sections, ys, ws, chunk, halves = sizes
    block = 4 * ys * ws
    length = BLOCKS * block
    chunks = length // chunk
    per_block = block // chunk
    per_half = per_block // halves
    ysub = ys // halves
    zs = ws // 2
    width = 2 * P_SIZE
    wide = ws * width
    sec = lax.axis_index("section")
    pos = lax.axis_index("tensor")
    y = pos // ws
    w = pos % ws
    z = w // 2
    core = w % 2
    top = sections - 1
    first_helper = sections - BLOCKS
    last_block = BLOCKS - 1
    downward = range(BLOCKS - 1, -1, -1)

    def remote(src, dst, send, recv, section, tensor):
        return pltpu.make_async_remote_copy(
            src_ref=src,
            dst_ref=dst,
            send_sem=send,
            recv_sem=recv,
            device_id=(section, tensor),
            device_id_type=pl.DeviceIdType.MESH,
        )

    def wait_bytes(like, sem):
        pltpu.make_async_copy(like, like, sem).wait()

    def columns(of, size):
        return pl.ds(pl.multiple_of(of * size, size), size)

    def to_y(d):
        return lax.rem(y + d, ys)

    def to_w(d):
        return lax.rem(w + d, ws)

    def at_y(d):
        return to_y(d) * ws + w

    def at_w(d):
        return y * ws + to_w(d)

    sibling = y * ws + z * 2 + (1 - core)
    below = lax.rem(sec + sections - 1, sections)

    fetches = [
        pltpu.make_async_copy(src, dst, in_sem.at[i])
        for i, (src, dst) in enumerate(
            (
                (act_ref, act_in),
                (taps_ref, taps_in),
                (step_ref, step_in),
                (rate_ref, rate_in),
                (skip_ref, skip_in),
            )
        )
    ]

    barrier = pltpu.get_barrier_semaphore()

    def greet(section, tensor):
        pl.semaphore_signal(
            barrier, inc=1, device_id=(section, tensor), device_id_type=pl.DeviceIdType.MESH
        )

    for d in range(1, ys):
        greet(sec, at_y(d))
    for d in range(1, ws):
        greet(sec, at_w(d))
    for d in range(1, sections):
        greet(lax.rem(sec + d, sections), pos)
    for fetch in fetches:
        fetch.start()
    pl.semaphore_wait(barrier, ys + ws + sections - 3)

    def bc1(which, d):
        return remote(
            (b_ref, c_ref)[which].at[:, :, columns(to_y(d), N)],
            bc_rows.at[y, :, which],
            bc1_s.at[0],
            bc1_r.at[0],
            sec,
            at_y(d),
        )

    for d in range(1, ys):
        for which in range(2):
            bc1(which, d).start()
    for which in range(2):
        pltpu.make_async_copy(
            (b_ref, c_ref)[which].at[:, :, columns(y, N)], bc_rows.at[y, :, which], bc1_r.at[0]
        ).start()

    helper = sec >= first_helper
    top_at = lax.max(sec - first_helper, 0)

    def top1(d):
        return remote(
            top_ref.at[top_at, :, columns(to_y(d), wide)],
            top_rows.at[y],
            top_s.at[0],
            top1_r.at[0],
            sec,
            at_y(d),
        )

    def top2(d):
        return remote(
            top_rows.at[:, :, columns(to_w(d), width)],
            top_all.at[:, w],
            top_s.at[1],
            top2_r.at[0],
            sec,
            at_w(d),
        )

    def top3(part):
        return remote(
            top_block.at[pl.ds(part * chunk, chunk), :],
            dy.at[pl.ds(pl.multiple_of(top_at * block + part * chunk, chunk), chunk), :],
            top_s.at[2],
            hop_r.at[top_at * per_block + part],
            top,
            pos,
        )

    @pl.when(helper)
    def _():
        for d in range(1, ys):
            top1(d).start()
        pltpu.make_async_copy(
            top_ref.at[top_at, :, columns(y, wide)], top_rows.at[y], top1_r.at[0]
        ).start()

    def bc2(at, d):
        to = sibling if d == 0 else y * ws + lax.rem(z + d, zs) * 2 + core
        recv = bc3_r if d == 0 else bc2_r
        return remote(bc_rows.at[:, at], bc_all.at[at, :, w], bc2_s.at[0], recv.at[at], sec, to)

    def bc3(at, d):
        piece = bc_all.at[at, :, lax.rem(z + zs - d, zs) * 2 + core]
        return remote(piece, piece, bc2_s.at[0], bc3_r.at[at], sec, sibling)

    wait_bytes(bc_rows, bc1_r.at[0])

    def spread(at):
        for d in range(zs - 1, -1, -1):
            bc2(at, d).start()
        pltpu.make_async_copy(bc_rows.at[:, at], bc_all.at[at, :, w], bc3_r.at[at]).start()

    spread(last_block)

    @pl.when(helper)
    def _():
        wait_bytes(top_rows, top1_r.at[0])
        for d in range(1, ws):
            top2(d).start()
        pltpu.make_async_copy(
            top_rows.at[:, :, columns(w, width)], top_all.at[:, w], top2_r.at[0]
        ).start()

    paced = sec >= PACED * sections // 8
    spread(last_block - 1)

    @pl.when(jnp.logical_not(paced))
    def _():
        for at in range(last_block - 2, -1, -1):
            spread(at)

    for fetch in fetches:
        fetch.wait()
    act_pad[0:PAD, :] = jnp.zeros((PAD, width), F32)
    act_pad[PAD:, :] = act_in[...].astype(F32)
    taps = taps_in[...].astype(F32)
    first = lax.broadcasted_iota(jnp.int32, (1, width), 1) < P_SIZE
    rate = jnp.where(first, rate_in[:, 0:1], rate_in[:, 1:2])
    skip = jnp.where(first, skip_in[:, 0:1], skip_in[:, 1:2])
    row_at = lax.broadcasted_iota(jnp.int32, (chunk, chunk), 0)
    col_at = lax.broadcasted_iota(jnp.int32, (chunk, chunk), 1)
    lower = (row_at >= col_at).astype(F32).astype(BF16)
    for at in range(chunks):
        rows = slice(at * chunk, (at + 1) * chunk)
        preact = jnp.zeros((chunk, width), F32)
        for k in range(K):
            start = PAD + at * chunk - k
            preact = preact + taps[k : k + 1] * act_pad[start : start + chunk, :]
        logistic = 1.0 / (1.0 + jnp.exp(-preact))
        slope_here = logistic * (1.0 + preact * (1.0 - logistic))
        step = jnp.concatenate(
            [jnp.broadcast_to(step_in[h : h + 1, rows], (P_SIZE, chunk)) for h in range(2)], axis=0
        ).T
        high = step.astype(BF16)
        rest = step - high.astype(F32)
        mid = rest.astype(BF16)
        low = (rest - mid.astype(F32)).astype(BF16)
        decay = -rate * (dot(lower, high) + dot(lower, mid) + dot(lower, low))
        grow[rows, :] = jnp.exp(decay)
        shrink[rows, :] = step * jnp.exp(-decay) * slope_here
        slope[rows, :] = skip * slope_here
    carried[...] = jnp.zeros_like(carried)
    extended[length:, :] = jnp.zeros((PAD, width), F32)

    @pl.when(helper)
    def _():
        wait_bytes(top_all, top2_r.at[0])
        gathered = top_all[...].reshape(block, width)

        @pl.when(sec == top)
        def _():
            dy[last_block * block :, :] = gathered

        @pl.when(sec != top)
        def _():
            top_block[...] = gathered
            for part in range(per_block - 1, -1, -1):
                top3(part).start()

    def hop(at):
        rows = pl.ds(at * chunk, chunk)
        return remote(
            stream.at[rows, :], dy.at[rows, :], hop_s.at[0], hop_r.at[at], below, pos
        )

    def out1(at, half, d):
        group = pl.ds(half * ysub, ysub)
        return remote(
            out_send.at[at, group, to_w(d)],
            out_rows.at[at, group, :, columns(w, width)],
            out1_s.at[0],
            out1_r.at[at * halves + half],
            sec,
            at_w(d),
        )

    def out2(at, half, d):
        to = half * ysub + lax.rem(y + d, ysub)
        return remote(
            out_rows.at[at, to],
            out_ref.at[at, :, columns(y, wide)],
            out2_s.at[0],
            out2_r.at[0],
            sec,
            to * ws + w,
        )

    def start_rows(at, half):
        group = pl.ds(half * ysub, ysub)
        begin = at * block + half * (block // halves)
        out_send[at, half * ysub : (half + 1) * ysub] = stream[
            begin : begin + block // halves, :
        ].reshape(ysub, ws, 4, width)
        for d in range(1, ws):
            out1(at, half, d).start()
        pltpu.make_async_copy(
            out_send.at[at, group, w],
            out_rows.at[at, group, :, columns(w, width)],
            out1_r.at[at * halves + half],
        ).start()

    def forward_rows(at, half):
        wait_bytes(out_rows.at[at, pl.ds(half * ysub, ysub)], out1_r.at[at * halves + half])
        for d in range(1, ysub):
            out2(at, half, d).start()
        mine = y // ysub == half

        @pl.when(mine)
        def _():
            pltpu.make_async_copy(
                out_rows.at[at, y], out_ref.at[at, :, columns(y, wide)], out2_r.at[0]
            ).start()

        @pl.when(jnp.logical_not(mine))
        def _():
            out2(at, half, 0).start()

    units = [(at, half) for at in downward for half in range(halves - 1, -1, -1)]
    done = 0
    for at in downward:
        wait_bytes(bc_all.at[at, :, 0 : zs - 1], bc2_r.at[at])
        if at >= 2:

            @pl.when(paced)
            def _():
                spread(at - 2)

        for d in range(1, zs):
            bc3(at, d).start()
        wait_bytes(bc_all.at[at, :, 0 : zs + 1], bc3_r.at[at])
        start = at * block
        b_flat[start : start + block, :] = bc_all[at, :, :, 0].reshape(block, N)
        c_here = bc_all[at, :, :, 1].reshape(block, N)
        for part in range(per_block):
            inner = slice(part * chunk, (part + 1) * chunk)
            rows = slice(start + part * chunk, start + (part + 1) * chunk)
            product = lax.dot_general(
                b_flat[rows, :], c_here[inner], (((1,), (1,)), ((), ())), preferred_element_type=F32
            )
            scores[rows, :] = jnp.where(col_at >= row_at, product, 0.0).astype(BF16)
            c_turned[at * per_block + part] = c_here[inner].T

        for part in range(per_block - 1, -1, -1):
            here = at * per_block + part
            rows = slice(here * chunk, (here + 1) * chunk)
            ended = grow[(here + 1) * chunk - 1 : (here + 1) * chunk, :] * carried[...]
            through = dot(b_flat[rows, :], ended.astype(BF16))

            if at == last_block:

                @pl.when(sec != top)
                def _():
                    hop(here).wait_recv()

            else:
                hop(here).wait_recv()

            upstream = dy[rows, :].astype(F32)
            fed = (grow[rows, :] * upstream).astype(BF16)
            mixed = dot(scores[rows, :], fed) + through
            grad_pre = shrink[rows, :] * mixed + slope[rows, :] * upstream
            extended[rows, :] = grad_pre
            grad_in = taps[0:1] * grad_pre
            for k in range(1, K):
                begin = here * chunk + k
                grad_in = grad_in + taps[k : k + 1] * extended[begin : begin + chunk, :]
            stream[rows, :] = (upstream + grad_in.astype(BF16).astype(F32)).astype(BF16)

            @pl.when(sec > 0)
            def _():
                hop(here).start()

            carried[...] = ended + dot(c_turned[here], fed)
            if part % per_half == 0:
                done += 1

                @pl.when(sec < EARLY)
                def _():
                    start_rows(*units[done - 1])
                    if done > LAG:
                        forward_rows(*units[done - 1 - LAG])

    @pl.when(sec >= EARLY)
    def _():
        for unit in units:
            start_rows(*unit)
        for unit in units[:-LAG]:
            forward_rows(*unit)

    conv = [jnp.zeros((1, width), F32) for _ in range(K)]
    for at in range(chunks):
        for k in range(K):
            start = PAD + at * chunk - k
            conv[k] = conv[k] + jnp.sum(
                extended[at * chunk : (at + 1) * chunk, :] * act_pad[start : start + chunk, :],
                axis=0,
                keepdims=True,
            )
    for k in range(K):
        conv_ref[k : k + 1, :] = conv[k]
    for unit in units[-LAG:]:
        forward_rows(*unit)

    wait_bytes(bc_rows.at[0 : ys - 1], bc1_s.at[0])
    wait_bytes(bc_all.at[:, :, 0 : 2 * zs - 1], bc2_s.at[0])

    @pl.when(helper)
    def _():
        wait_bytes(top_rows.at[0 : ys - 1], top_s.at[0])
        wait_bytes(top_all.at[:, 0 : ws - 1], top_s.at[1])

    @pl.when(helper & (sec != top))
    def _():
        wait_bytes(top_block, top_s.at[2])

    @pl.when(sec > 0)
    def _():
        wait_bytes(stream, hop_s.at[0])

    wait_bytes(out_send.at[:, :, 0 : ws - 1], out1_s.at[0])
    for at in range(BLOCKS):
        wait_bytes(out_rows.at[at, 0 : ys - 1], out2_s.at[0])
    wait_bytes(out_ref, out2_r.at[0])


def on_device(
    activations, conv_weight, step_size, decay_rate, skip_gain, b_matrix, c_matrix, top_grad
):
    tensor_size = lax.axis_size("tensor")
    sections = lax.axis_size("section")
    ys = b_matrix.shape[-1] // N
    ws = tensor_size // ys
    length, width = activations.shape[1:]
    chunk = min(CHUNK, length // BLOCKS)
    chunks = length // chunk
    halves = min(HALVES, length // BLOCKS // chunk)
    dma = pltpu.SemaphoreType.DMA
    out, conv = pl.pallas_call(
        functools.partial(kernel, (sections, ys, ws, chunk, halves)),
        out_shape=(
            jax.ShapeDtypeStruct(top_grad.shape, BF16),
            jax.ShapeDtypeStruct((K, width), F32),
        ),
        in_specs=[pl.BlockSpec(memory_space=pltpu.HBM)] * 8,
        out_specs=(pl.BlockSpec(memory_space=pltpu.VMEM),) * 2,
        scratch_shapes=[
            pltpu.VMEM((length, width), BF16),
            pltpu.VMEM((K, width), BF16),
            pltpu.VMEM((2, length), F32),
            pltpu.VMEM((1, 2), F32),
            pltpu.VMEM((1, 2), F32),
            pltpu.VMEM((ys, BLOCKS, 2, 4, N), BF16),
            pltpu.VMEM((BLOCKS, ys, ws, 2, 4, N), BF16),
            pltpu.VMEM((ys, 4, ws * width), BF16),
            pltpu.VMEM((ys, ws, 4, width), BF16),
            pltpu.VMEM((length // BLOCKS, width), BF16),
            pltpu.VMEM((PAD + length, width), F32),
            pltpu.VMEM((length, width), F32),
            pltpu.VMEM((length, width), F32),
            pltpu.VMEM((length, width), F32),
            pltpu.VMEM((length, N), BF16),
            pltpu.VMEM((chunks, N, chunk), BF16),
            pltpu.VMEM((length, chunk), BF16),
            pltpu.VMEM((N, width), F32),
            pltpu.VMEM((length, width), BF16),
            pltpu.VMEM((length, width), BF16),
            pltpu.VMEM((length + PAD, width), F32),
            pltpu.VMEM((BLOCKS, ys, ws, 4, width), BF16),
            pltpu.VMEM((BLOCKS, ys, 4, ws * width), BF16),
            dma((5,)),
            dma((1,)),
            dma((1,)),
            dma((1,)),
            dma((BLOCKS,)),
            dma((BLOCKS,)),
            dma((3,)),
            dma((1,)),
            dma((1,)),
            dma((1,)),
            dma((chunks,)),
            dma((1,)),
            dma((BLOCKS * halves,)),
            dma((1,)),
            dma((1,)),
        ],
        compiler_params=pltpu.CompilerParams(
            collective_id=0, has_side_effects=True, vmem_limit_bytes=60 * 1024 * 1024
        ),
    )(
        activations[0],
        conv_weight[0],
        step_size[0].T,
        decay_rate,
        skip_gain,
        b_matrix[0],
        c_matrix[0],
        top_grad,
    )
    return (out[None], conv[None])


def solution(mesh):
    return jax.shard_map(
        on_device,
        mesh=mesh,
        in_specs=(
            P("section", None, "tensor"),
            P("section", None, "tensor"),
            P("section", None, "tensor"),
            P("section", "tensor"),
            P("section", "tensor"),
            P("section", None, "tensor", None),
            P("section", None, "tensor", None),
            P(None, "tensor", None),
        ),
        out_specs=(P("section", None, "tensor", None), P("section", None, "tensor")),
        check_vma=False,
    )
```

time: 867 us -> 79.1 us (0.09); the launches traced: 855 us -> 78.9 us
  waiting for transfers between devices: 439 us -> 0 us
  local copies, waits for them, and re-layouts: 306 us -> 2.33 us
  Pallas kernels: 0 us -> 76 us
  starting transfers between devices: 70.2 us -> 0 us
  other arithmetic: 22.6 us -> 0 us
  matrix products: 13.6 us -> 0 us
    ppermute x7 -> x0, waiting for transfers between devices: 428 us -> none  [passed_along(): return lax.ppermute(array, axis, pairs)]
    unnamed x43 -> x4, local copies, waits for them, and re-layouts: 185 us -> 2.33 us
    pallas_call x0 -> x1, Pallas kernels: none -> 76 us  [on_device(): pl.pallas_call(functools.partial(kernel, (sections, ys, ws, chunk, halves...]
    all_to_all x4 -> x0, starting transfers between devices: 61.3 us -> none  [the longest x1 24.9 us: on_device(): lax.all_to_all(as_sent(stream_heads), 'tensor', split_axis=1, concat_axis...]
    all_to_all x6 -> x0, local copies, waits for them, and re-layouts: 56.2 us -> none  [the longest x2 23 us: on_device(): lax.all_to_all(widen_groups(b_matrix), 'tensor', split_axis=2, concat_axi...]
    cond x8 -> x0, local copies, waits for them, and re-layouts: 13.7 us -> none  [on_device(): lax.cond(active, whole_layer, pass_through, upstream)]
    dot_general x14 -> x0, matrix products: 13.6 us -> none  [the longest x4 5.77 us: block_back(): jnp.einsum('hji,jhp->ihp', weight, grad_heads, preferred_element_type=jnp...]
    select_n x8 -> x0, local copies, waits for them, and re-layouts: 13.5 us -> none  [the longest x7 12.6 us: on_device(): upstream = jnp.where(section_pos == section_count - 1, grad_top, received)]
  transfers between devices with their start and end apart: 11 -> 0, of which waited for: 8 -> 0; matrix products, arithmetic and copies ran while one was open for 21% -> 0% of each run, Pallas kernels for 0% -> 0%
where the time goes in v2:
time: 79.1 us; the launch traced here: 78.9 us
  Pallas kernels  76 us (96%)
  local copies, waits for them, and re-layouts  2.33 us (3%)
    pallas_call x1, Pallas kernels, on_device(): pl.pallas_call(functools.partial(kernel, (sections, ys, ws, chunk, halves...  76 us
    unnamed x4, local copies, waits for them, and re-layouts  2.33 us

profile of v2, /device:TPU:1, one launch (start us, length us, event | category | flops | bytes accessed | tf_op | source)
XLA Modules:
  0.0 78.9 jit_solution(1546855500862587284)
XLA Ops:
  0.6 76.0 %shard_map.95 = (bf16[4,4,8192]{2,1,0:T(4,128)(2,1)}, f32[4,128]{1,0:T(4,128)}) custom-call(bf16[1024,128]{1,0:T(8,128)(2,1)} %bitcast.10, bf16[4,128]{1,0:T(4,128)(2,1)} %bitcast.15, f32[2,1024]{1,0:T(2,128)} %bitcast.13, f32[1,2]{1,0:T(1,128)} %rate_ref.1, f32[1,2]{1,0:T(1,128)} %skip_ref.1, bf16[4,4,2048]{2,1,0:T(4,128)(2,1)} %bitcast.11, ...), custom_call_target="tpu_custom_call" | custom-call | tf_op jit(solution)/shard_map/pallas_call | solution.py:481
  76.6 0.0 copy-start
  76.6 1.7 %copy.12 = bf16[1,4,4,8192]{3,2,1,0:T(4,128)(2,1)} copy(bf16[1,4,4,8192]{3,2,1,0:T(4,128)(2,1)} %bitcast.9) | data formatting | bytes 524288
  78.4 0.0 copy-done
  78.4 0.6 copy.13
Async XLA Ops:
  76.6 1.8 %copy-start = (f32[4,128]{1,0:T(4,128)S(1)}, f32[4,128]{1,0:T(4,128)}, u32[]{:S(2)}) copy-start(f32[4,128]{1,0:T(4,128)} %get-tuple-element.5) | copy-start | bytes 6148

commit v3 on v2

--- a/solution.py
+++ b/solution.py
@@ -11,7 +11,7 @@
 N = 256
 K = 4
 BLOCKS = 4
-CHUNK = 128
+CHUNK = 64
 HALVES = 2
 EARLY = 3
 LAG = 3
@@ -75,6 +75,8 @@
     out1_r,
     out2_s,
     out2_r,
+    out3_s,
+    ready,
 ):
     sections, ys, ws, chunk, halves = sizes
     block = 4 * ys * ws
@@ -93,7 +95,6 @@
     z = w // 2
     core = w % 2
     top = sections - 1
-    first_helper = sections - BLOCKS
     last_block = BLOCKS - 1
     downward = range(BLOCKS - 1, -1, -1)
 
@@ -152,32 +153,31 @@
         greet(sec, at_y(d))
     for d in range(1, ws):
         greet(sec, at_w(d))
-    for d in range(1, sections):
-        greet(lax.rem(sec + d, sections), pos)
+
+    @pl.when(sec < top)
+    def _():
+        greet(sec + 1, pos)
+
+    @pl.when(sec < BLOCKS)
+    def _():
+        greet(top, pos)
+
     for fetch in fetches:
         fetch.start()
-    pl.semaphore_wait(barrier, ys + ws + sections - 3)
-
-    def bc1(which, d):
-        return remote(
-            (b_ref, c_ref)[which].at[:, :, columns(to_y(d), N)],
-            bc_rows.at[y, :, which],
-            bc1_s.at[0],
-            bc1_r.at[0],
-            sec,
-            at_y(d),
-        )
-
-    for d in range(1, ys):
-        for which in range(2):
-            bc1(which, d).start()
-    for which in range(2):
-        pltpu.make_async_copy(
-            (b_ref, c_ref)[which].at[:, :, columns(y, N)], bc_rows.at[y, :, which], bc1_r.at[0]
-        ).start()
-
-    helper = sec >= first_helper
-    top_at = lax.max(sec - first_helper, 0)
+    below_greets = jnp.where(sec > 0, 1, 0)
+    helpers_greet = jnp.where(sec == top, BLOCKS, 0)
+    pl.semaphore_wait(barrier, ys + ws - 2 + below_greets + helpers_greet)
+
+    @pl.when(sec == top)
+    def _():
+        for to in range(BLOCKS):
+            pl.semaphore_signal(
+                ready.at[0], inc=1, device_id=(to, pos), device_id_type=pl.DeviceIdType.MESH
+            )
+
+
+    helper = sec < BLOCKS
+    top_at = jnp.where(sec == 3, 0, jnp.where(sec == 2, 3, jnp.where(sec == 1, 1, 2)))
 
     def top1(d):
         return remote(
@@ -217,23 +217,26 @@
             top_ref.at[top_at, :, columns(y, wide)], top_rows.at[y], top1_r.at[0]
         ).start()
 
-    def bc2(at, d):
-        to = sibling if d == 0 else y * ws + lax.rem(z + d, zs) * 2 + core
-        recv = bc3_r if d == 0 else bc2_r
-        return remote(bc_rows.at[:, at], bc_all.at[at, :, w], bc2_s.at[0], recv.at[at], sec, to)
-
-    def bc3(at, d):
-        piece = bc_all.at[at, :, lax.rem(z + zs - d, zs) * 2 + core]
-        return remote(piece, piece, bc2_s.at[0], bc3_r.at[at], sec, sibling)
-
-    wait_bytes(bc_rows, bc1_r.at[0])
-
-    def spread(at):
-        for d in range(zs - 1, -1, -1):
-            bc2(at, d).start()
-        pltpu.make_async_copy(bc_rows.at[:, at], bc_all.at[at, :, w], bc3_r.at[at]).start()
-
-    spread(last_block)
+    def bc1(at, which, d):
+        return remote(
+            (b_ref, c_ref)[which].at[at, :, columns(to_y(d), N)],
+            bc_rows.at[y, at, which],
+            bc1_s.at[0],
+            bc1_r.at[at],
+            sec,
+            at_y(d),
+        )
+
+    for at in downward:
+        for d in range(1, ys):
+            for which in range(2):
+                bc1(at, which, d).start()
+        for which in range(2):
+            pltpu.make_async_copy(
+                (b_ref, c_ref)[which].at[at, :, columns(y, N)],
+                bc_rows.at[y, at, which],
+                bc1_r.at[at],
+            ).start()
 
     @pl.when(helper)
     def _():
@@ -244,13 +247,36 @@
             top_rows.at[:, :, columns(w, width)], top_all.at[:, w], top2_r.at[0]
         ).start()
 
+    def bc2(at, d):
+        to = sibling if d == 0 else y * ws + lax.rem(z + d, zs) * 2 + core
+        recv = bc3_r if d == 0 else bc2_r
+        return remote(bc_rows.at[:, at], bc_all.at[at, :, w], bc2_s.at[0], recv.at[at], sec, to)
+
+    def bc3(at, d):
+        piece = bc_all.at[at, :, lax.rem(z + zs - d, zs) * 2 + core]
+        return remote(piece, piece, bc2_s.at[0], bc3_r.at[at], sec, sibling)
+
+    def spread(at):
+        for d in range(zs - 1, -1, -1):
+            bc2(at, d).start()
+        pltpu.make_async_copy(bc_rows.at[:, at], bc_all.at[at, :, w], bc3_r.at[at]).start()
+
     paced = sec >= PACED * sections // 8
-    spread(last_block - 1)
-
-    @pl.when(jnp.logical_not(paced))
-    def _():
-        for at in range(last_block - 2, -1, -1):
-            spread(at)
+
+    def collect(at):
+        wait_bytes(bc_all.at[at, :, 0 : zs - 1], bc2_r.at[at])
+
+        if at >= 2:
+
+            @pl.when(paced)
+            def _():
+                spread(at - 2)
+
+        for d in range(1, zs):
+            bc3(at, d).start()
+
+    wait_bytes(bc_rows.at[:, last_block], bc1_r.at[last_block])
+    spread(last_block)
 
     for fetch in fetches:
         fetch.wait()
@@ -285,20 +311,30 @@
     carried[...] = jnp.zeros_like(carried)
     extended[length:, :] = jnp.zeros((PAD, width), F32)
 
+    wait_bytes(bc_rows.at[:, last_block - 1], bc1_r.at[last_block - 1])
+    spread(last_block - 1)
+    for at in range(last_block - 2, -1, -1):
+        wait_bytes(bc_rows.at[:, at], bc1_r.at[at])
+
+    @pl.when(jnp.logical_not(paced))
+    def _():
+        for at in range(last_block - 2, -1, -1):
+            spread(at)
+
     @pl.when(helper)
     def _():
         wait_bytes(top_all, top2_r.at[0])
         gathered = top_all[...].reshape(block, width)
 
-        @pl.when(sec == top)
-        def _():
-            dy[last_block * block :, :] = gathered
-
-        @pl.when(sec != top)
-        def _():
-            top_block[...] = gathered
-            for part in range(per_block - 1, -1, -1):
-                top3(part).start()
+        top_block[...] = gathered
+        pl.semaphore_wait(ready.at[0], 1)
+        for part in range(per_block - 1, -1, -1):
+            top3(part).start()
+
+    @pl.when(jnp.logical_not(paced))
+    def _():
+        for at in downward:
+            collect(at)
 
     def hop(at):
         rows = pl.ds(at * chunk, chunk)
@@ -327,6 +363,32 @@
             sec,
             to * ws + w,
         )
+
+    def out3(to, d):
+        return remote(
+            out_send.at[0, to, to_w(d)],
+            out_ref.at[0, :, columns(pos, width)],
+            out3_s.at[0 if d else 1],
+            out2_r.at[0],
+            sec,
+            to * ws + to_w(d),
+        )
+
+    def send_last():
+        out_send[0, 0:ysub] = stream[0 : block // halves, :].reshape(ysub, ws, 4, width)
+        for to in range(ysub):
+            for d in range(1, ws):
+                out3(to, d).start()
+
+            @pl.when(y == to)
+            def _():
+                pltpu.make_async_copy(
+                    out_send.at[0, to, w], out_ref.at[0, :, columns(pos, width)], out2_r.at[0]
+                ).start()
+
+            @pl.when(y != to)
+            def _():
+                out3(to, 0).start()
 
     def start_rows(at, half):
         group = pl.ds(half * ysub, ysub)
@@ -361,15 +423,10 @@
     units = [(at, half) for at in downward for half in range(halves - 1, -1, -1)]
     done = 0
     for at in downward:
-        wait_bytes(bc_all.at[at, :, 0 : zs - 1], bc2_r.at[at])
-        if at >= 2:
-
-            @pl.when(paced)
-            def _():
-                spread(at - 2)
-
-        for d in range(1, zs):
-            bc3(at, d).start()
+        @pl.when(paced)
+        def _():
+            collect(at)
+
         wait_bytes(bc_all.at[at, :, 0 : zs + 1], bc3_r.at[at])
         start = at * block
         b_flat[start : start + block, :] = bc_all[at, :, :, 0].reshape(block, N)
@@ -389,15 +446,7 @@
             ended = grow[(here + 1) * chunk - 1 : (here + 1) * chunk, :] * carried[...]
             through = dot(b_flat[rows, :], ended.astype(BF16))
 
-            if at == last_block:
-
-                @pl.when(sec != top)
-                def _():
-                    hop(here).wait_recv()
-
-            else:
-                hop(here).wait_recv()
-
+            hop(here).wait_recv()
             upstream = dy[rows, :].astype(F32)
             fed = (grow[rows, :] * upstream).astype(BF16)
             mixed = dot(scores[rows, :], fed) + through
@@ -419,16 +468,23 @@
 
                 @pl.when(sec < EARLY)
                 def _():
-                    start_rows(*units[done - 1])
+                    if done < len(units):
+                        start_rows(*units[done - 1])
+                    else:
+                        send_last()
                     if done > LAG:
                         forward_rows(*units[done - 1 - LAG])
 
     @pl.when(sec >= EARLY)
     def _():
-        for unit in units:
+        for unit in units[:-1]:
             start_rows(*unit)
+        send_last()
         for unit in units[:-LAG]:
             forward_rows(*unit)
+
+    for unit in units[-LAG:-1]:
+        forward_rows(*unit)
 
     conv = [jnp.zeros((1, width), F32) for _ in range(K)]
     for at in range(chunks):
@@ -441,8 +497,6 @@
             )
     for k in range(K):
         conv_ref[k : k + 1, :] = conv[k]
-    for unit in units[-LAG:]:
-        forward_rows(*unit)
 
     wait_bytes(bc_rows.at[0 : ys - 1], bc1_s.at[0])
     wait_bytes(bc_all.at[:, :, 0 : 2 * zs - 1], bc2_s.at[0])
@@ -451,18 +505,29 @@
     def _():
         wait_bytes(top_rows.at[0 : ys - 1], top_s.at[0])
         wait_bytes(top_all.at[:, 0 : ws - 1], top_s.at[1])
-
-    @pl.when(helper & (sec != top))
-    def _():
         wait_bytes(top_block, top_s.at[2])
 
     @pl.when(sec > 0)
     def _():
         wait_bytes(stream, hop_s.at[0])
 
-    wait_bytes(out_send.at[:, :, 0 : ws - 1], out1_s.at[0])
-    for at in range(BLOCKS):
+    wait_bytes(out_send.at[1:BLOCKS, :, 0 : ws - 1], out1_s.at[0])
+    wait_bytes(out_send.at[0, ysub:ys, 0 : ws - 1], out1_s.at[0])
+    for at in range(1, BLOCKS):
         wait_bytes(out_rows.at[at, 0 : ys - 1], out2_s.at[0])
+    wait_bytes(out_send.at[0, 0:ysub, 0 : ws - 1], out3_s.at[0])
+    in_last = y // ysub == 0
+
+    @pl.when(in_last)
+    def _():
+        wait_bytes(out_rows.at[0, 0 : ys - ysub], out2_s.at[0])
+        wait_bytes(out_send.at[0, 0 : ysub - 1, 0], out3_s.at[1])
+
+    @pl.when(jnp.logical_not(in_last))
+    def _():
+        wait_bytes(out_rows.at[0, 0 : ysub - 1], out2_s.at[0])
+        wait_bytes(out_send.at[0, 0:ysub, 0], out3_s.at[1])
+
     wait_bytes(out_ref, out2_r.at[0])
 
 
@@ -512,7 +577,7 @@
             pltpu.VMEM((BLOCKS, ys, 4, ws * width), BF16),
             dma((5,)),
             dma((1,)),
-            dma((1,)),
+            dma((BLOCKS,)),
             dma((1,)),
             dma((BLOCKS,)),
             dma((BLOCKS,)),
@@ -525,6 +590,8 @@
             dma((BLOCKS * halves,)),
             dma((1,)),
             dma((1,)),
+            dma((2,)),
+            pltpu.SemaphoreType.REGULAR((1,)),
         ],
         compiler_params=pltpu.CompilerParams(
             collective_id=0, has_side_effects=True, vmem_limit_bytes=60 * 1024 * 1024

time: 79.1 us -> 75.6 us (0.956)
  Pallas kernels: 76 us -> 72.5 us
    pallas_call x1, Pallas kernels: 76 us -> 72.5 us  [on_device(): pl.pallas_call(functools.partial(kernel, (sections, ys, ws, chunk, halves...]
where the time goes in v3:
time: 75.6 us; the launch traced here: 75.5 us
  Pallas kernels  72.5 us (96%)
  local copies, waits for them, and re-layouts  2.33 us (3%)
    pallas_call x1, Pallas kernels, on_device(): pl.pallas_call(functools.partial(kernel, (sections, ys, ws, chunk, halves...  72.5 us
    unnamed x4, local copies, waits for them, and re-layouts  2.33 us

profile of v3, /device:TPU:1, one launch (start us, length us, event | category | flops | bytes accessed | tf_op | source)
XLA Modules:
  0.0 75.5 jit_solution(12231854698500451794)
XLA Ops:
  0.6 72.5 %shard_map.95 = (bf16[4,4,8192]{2,1,0:T(4,128)(2,1)}, f32[4,128]{1,0:T(4,128)}) custom-call(bf16[1024,128]{1,0:T(8,128)(2,1)} %bitcast.10, bf16[4,128]{1,0:T(4,128)(2,1)} %bitcast.15, f32[2,1024]{1,0:T(2,128)} %bitcast.13, f32[1,2]{1,0:T(1,128)} %rate_ref.1, f32[1,2]{1,0:T(1,128)} %skip_ref.1, bf16[4,4,2048]{2,1,0:T(4,128)(2,1)} %bitcast.11, ...), custom_call_target="tpu_custom_call" | custom-call | tf_op jit(solution)/shard_map/pallas_call | solution.py:546
  73.1 0.0 copy-start
  73.1 1.7 %copy.12 = bf16[1,4,4,8192]{3,2,1,0:T(4,128)(2,1)} copy(bf16[1,4,4,8192]{3,2,1,0:T(4,128)(2,1)} %bitcast.9) | data formatting | bytes 524288
  74.9 0.0 copy-done
  74.9 0.6 copy.13
Async XLA Ops:
  73.1 1.8 %copy-start = (f32[4,128]{1,0:T(4,128)S(1)}, f32[4,128]{1,0:T(4,128)}, u32[]{:S(2)}) copy-start(f32[4,128]{1,0:T(4,128)} %get-tuple-element.5) | copy-start | bytes 6148

commit v4 on v3

--- a/solution.py
+++ b/solution.py
@@ -525,7 +525,7 @@
 
     @pl.when(jnp.logical_not(in_last))
     def _():
-        wait_bytes(out_rows.at[0, 0 : ysub - 1], out2_s.at[0])
+        wait_bytes(out_rows.at[0, 0 : ys - ysub - 1], out2_s.at[0])
         wait_bytes(out_send.at[0, 0:ysub, 0], out3_s.at[1])
 
     wait_bytes(out_ref, out2_r.at[0])
@@ -594,17 +594,22 @@
             pltpu.SemaphoreType.REGULAR((1,)),
         ],
         compiler_params=pltpu.CompilerParams(
-            collective_id=0, has_side_effects=True, vmem_limit_bytes=60 * 1024 * 1024
+            collective_id=0, has_side_effects=True, vmem_limit_bytes=40 * 1024 * 1024
         ),
     )(
-        activations[0],
-        conv_weight[0],
-        step_size[0].T,
-        decay_rate,
-        skip_gain,
-        b_matrix[0],
-        c_matrix[0],
-        top_grad,
+        *(
+            pltpu.with_memory_space_constraint(array, pltpu.HBM)
+            for array in (
+                activations[0],
+                conv_weight[0],
+                step_size[0].T,
+                decay_rate,
+                skip_gain,
+                b_matrix[0],
+                c_matrix[0],
+                top_grad,
+            )
+        )
     )
     return (out[None], conv[None])
 

time: 75.6 us -> 73.8 us (0.976)
  local copies, waits for them, and re-layouts: 2.33 us -> 1.28 us
    unnamed x4 -> x2, local copies, waits for them, and re-layouts: 2.33 us -> 1.28 us
where the time goes in v4:
time: 73.8 us; the launch traced here: 73.7 us
  Pallas kernels  71.8 us (97%)
  local copies, waits for them, and re-layouts  1.28 us (2%)
    pallas_call x1, Pallas kernels, on_device(): pl.pallas_call(functools.partial(kernel, (sections, ys, ws, chunk, halves...  71.8 us

profile of v4, /device:TPU:1, one launch (start us, length us, event | category | flops | bytes accessed | tf_op | source)
XLA Modules:
  0.0 73.7 jit_solution(6746893782806807515)
XLA Ops:
  0.6 71.8 %shard_map.95 = (bf16[4,4,8192]{2,1,0:T(4,128)(2,1)S(1)}, f32[4,128]{1,0:T(4,128)S(1)}) custom-call(bf16[1024,128]{1,0:T(8,128)(2,1)} %bitcast.11, bf16[4,128]{1,0:T(4,128)(2,1)} %bitcast.15, f32[2,1024]{1,0:T(2,128)} %bitcast.14, f32[1,2]{1,0:T(1,128)} %rate_ref.1, f32[1,2]{1,0:T(1,128)} %skip_ref.1, bf16[4,4,2048]{2,1,0:T(4,128)(2,1)} %bitcast.12, ...), custom_call_target="tpu_custom_call" | custom-call | tf_op jit(solution)/shard_map/pallas_call | solution.py:546
  72.4 0.7 copy.12
  73.1 0.6 copy.13

commit v5 on v4

--- a/solution.py
+++ b/solution.py
@@ -16,6 +16,7 @@
 EARLY = 3
 LAG = 3
 PACED = 6
+ROUND = (12, 10, 8, 6, 4)
 PAD = 8
 F32 = jnp.float32
 BF16 = jnp.bfloat16
@@ -58,6 +59,7 @@
     dy,
     stream,
     extended,
+    passing,
     out_send,
     out_rows,
     in_sem,
@@ -71,6 +73,8 @@
     top2_r,
     hop_s,
     hop_r,
+    pass_s,
+    pass_r,
     out1_s,
     out1_r,
     out2_s,
@@ -95,6 +99,7 @@
     z = w // 2
     core = w % 2
     top = sections - 1
+    crossing = sections // 2
     last_block = BLOCKS - 1
     downward = range(BLOCKS - 1, -1, -1)
 
@@ -342,6 +347,27 @@
             stream.at[rows, :], dy.at[rows, :], hop_s.at[0], hop_r.at[at], below, pos
         )
 
+    def round_out(at):
+        slot = ROUND.index(at)
+        return remote(
+            stream.at[pl.ds(at * chunk, chunk), :],
+            passing.at[slot],
+            hop_s.at[0],
+            pass_r.at[slot],
+            top,
+            pos,
+        )
+
+    def round_on(at):
+        return remote(
+            passing.at[ROUND.index(at)],
+            dy.at[pl.ds(at * chunk, chunk), :],
+            pass_s.at[0],
+            hop_r.at[at],
+            crossing - 1,
+            pos,
+        )
+
     def out1(at, half, d):
         group = pl.ds(half * ysub, ysub)
         return remote(
@@ -450,6 +476,7 @@
             upstream = dy[rows, :].astype(F32)
             fed = (grow[rows, :] * upstream).astype(BF16)
             mixed = dot(scores[rows, :], fed) + through
+            update = dot(c_turned[here], fed)
             grad_pre = shrink[rows, :] * mixed + slope[rows, :] * upstream
             extended[rows, :] = grad_pre
             grad_in = taps[0:1] * grad_pre
@@ -458,11 +485,24 @@
                 grad_in = grad_in + taps[k : k + 1] * extended[begin : begin + chunk, :]
             stream[rows, :] = (upstream + grad_in.astype(BF16).astype(F32)).astype(BF16)
 
-            @pl.when(sec > 0)
-            def _():
-                hop(here).start()
-
-            carried[...] = ended + dot(c_turned[here], fed)
+            if here in ROUND:
+
+                @pl.when((sec > 0) & (sec != crossing))
+                def _():
+                    hop(here).start()
+
+                @pl.when(sec == crossing)
+                def _():
+                    round_out(here).start()
+
+            else:
+
+                @pl.when(sec > 0)
+                def _():
+                    hop(here).start()
+
+            if here > 0:
+                carried[...] = ended + update
             if part % per_half == 0:
                 done += 1
 
@@ -474,6 +514,12 @@
                         send_last()
                     if done > LAG:
                         forward_rows(*units[done - 1 - LAG])
+
+    @pl.when(sec == top)
+    def _():
+        for slot, at in enumerate(ROUND):
+            wait_bytes(passing.at[slot], pass_r.at[slot])
+            round_on(at).start()
 
     @pl.when(sec >= EARLY)
     def _():
@@ -506,6 +552,10 @@
         wait_bytes(top_rows.at[0 : ys - 1], top_s.at[0])
         wait_bytes(top_all.at[:, 0 : ws - 1], top_s.at[1])
         wait_bytes(top_block, top_s.at[2])
+
+    @pl.when(sec == top)
+    def _():
+        wait_bytes(passing, pass_s.at[0])
 
     @pl.when(sec > 0)
     def _():
@@ -573,6 +623,7 @@
             pltpu.VMEM((length, width), BF16),
             pltpu.VMEM((length, width), BF16),
             pltpu.VMEM((length + PAD, width), F32),
+            pltpu.VMEM((len(ROUND), chunk, width), BF16),
             pltpu.VMEM((BLOCKS, ys, ws, 4, width), BF16),
             pltpu.VMEM((BLOCKS, ys, 4, ws * width), BF16),
             dma((5,)),
@@ -586,6 +637,8 @@
             dma((1,)),
             dma((1,)),
             dma((chunks,)),
+            dma((1,)),
+            dma((len(ROUND),)),
             dma((1,)),
             dma((BLOCKS * halves,)),
             dma((1,)),

time: 73.8 us -> 73.2 us (level)
  no operation moved by 1% of the time
where the time goes in v5:
time: 73.2 us; the launch traced here: 73.1 us
  Pallas kernels  71.1 us (97%)
  local copies, waits for them, and re-layouts  1.28 us (2%)
    pallas_call x1, Pallas kernels, on_device(): pl.pallas_call(functools.partial(kernel, (sections, ys, ws, chunk, halves...  71.1 us

profile of v5, /device:TPU:1, one launch (start us, length us, event | category | flops | bytes accessed | tf_op | source)
XLA Modules:
  0.0 73.1 jit_solution(8512407346651229885)
XLA Ops:
  0.6 71.1 %shard_map.95 = (bf16[4,4,8192]{2,1,0:T(4,128)(2,1)S(1)}, f32[4,128]{1,0:T(4,128)S(1)}) custom-call(bf16[1024,128]{1,0:T(8,128)(2,1)} %bitcast.11, bf16[4,128]{1,0:T(4,128)(2,1)} %bitcast.15, f32[2,1024]{1,0:T(2,128)} %bitcast.14, f32[1,2]{1,0:T(1,128)} %rate_ref.1, f32[1,2]{1,0:T(1,128)} %skip_ref.1, bf16[4,4,2048]{2,1,0:T(4,128)(2,1)} %bitcast.12, ...), custom_call_target="tpu_custom_call" | custom-call | tf_op jit(solution)/shard_map/pallas_call | solution.py:596
  71.8 0.7 copy.12
  72.5 0.6 copy.13
